TPU v7x, 128 devices: a whole 4x4x4 slice. The times are simulated.
128 devices in a mesh: orb: 16 (over y_lo, z, core), dom: 8 (over y_hi, x).
Axes of the slice: x: 4, y: 4 (y_hi: 2, y_lo: 2; y = y_hi * 2 + y_lo), z: 4, core: 2. Of those that a mesh axis runs over, the one named last changes fastest.
Arguments:
- orbitals: float32 [128, 64, 64, 128], P('orb', 'dom'), may hold values from -6 to 6
- veff: float32 [64, 64, 128], P('dom'), may hold values from -1 to 0
- trials: float32 [16, 64, 64, 128], P('orb', 'dom'), may hold values from -32 to 32
- owners: int32 [2], replicated, may hold values from 0 to 15
- levels: float32 [8], replicated, may hold values from 0.05 to 1
- shift_index: int32 [128], P('orb'), may hold values from 0 to 7
Outputs:
- responses: float32 [16, 64, 64, 128], P('orb', 'dom')
Inputs may be any that keep to these rules, and one draw needn't show every extreme that they name: `owners`: an orbital group index. `shift_index`: an index into levels.
All inputs are finite; a program needn't handle non-finite values.
Results may differ from a plain program's by a relative error of at most 0.0001.
Values sent between devices are 32-bit elements; how exact they have to be, the bound alone decides.
A program may use at most 128 MiB of HBM per device.

v0:
```python
import jax
import jax.numpy as jnp
from jax import lax
from jax.sharding import PartitionSpec as P

APPS = 2
SWEEPS = 4
stencil_taps = (-49.0 / 18.0, 1.5, -0.15, 1.0 / 90.0)
center_shift = 4.05
center_depth = 5.05
inverse_half = 1.0 / 5.05
norm_epsilon = 1e-06


def extended_2(block, sides, width):
    for axis, dim in sides:
        count = lax.axis_size(axis)
        forward = [(i, i + 1) for i in range(count - 1)]
        backward = [(target, source) for source, target in forward]
        low = lax.ppermute(
            lax.slice_in_dim(block, block.shape[dim] - width, None, axis=dim), axis, forward
        )
        high = lax.ppermute(lax.slice_in_dim(block, 0, width, axis=dim), axis, backward)
        block = jnp.concatenate([low, block, high], axis=dim)
    return block


def spread(shard, axis, root):
    mine = lax.axis_index(axis) == root
    return lax.psum(jnp.where(mine, shard, jnp.zeros_like(shard)), axis)


def apply_map(extended, potential_in):
    inner_count = extended.shape[1] - 6
    width_y = extended.shape[2]
    width_z = extended.shape[3]
    padded = jnp.pad(extended, ((0, 0), (0, 0), (3, 3), (3, 3)))
    middle = padded[:, 3 : 3 + inner_count, 3 : 3 + width_y, 3 : 3 + width_z]
    laplace = 3.0 * stencil_taps[0] * middle
    for offset in (1, 2, 3):
        weight = stencil_taps[offset]
        laplace = laplace + weight * (
            padded[:, 3 + offset : 3 + offset + inner_count, 3 : 3 + width_y, 3 : 3 + width_z]
            + padded[:, 3 - offset : 3 - offset + inner_count, 3 : 3 + width_y, 3 : 3 + width_z]
        )
        laplace = laplace + weight * (
            padded[:, 3 : 3 + inner_count, 3 + offset : 3 + offset + width_y, 3 : 3 + width_z]
            + padded[:, 3 : 3 + inner_count, 3 - offset : 3 - offset + width_y, 3 : 3 + width_z]
        )
        laplace = laplace + weight * (
            padded[:, 3 : 3 + inner_count, 3 : 3 + width_y, 3 + offset : 3 + offset + width_z]
            + padded[:, 3 : 3 + inner_count, 3 : 3 + width_y, 3 - offset : 3 - offset + width_z]
        )
    energy = -0.5 * laplace + potential_in[None] * middle
    return (energy - center_shift * middle) * inverse_half


def coefficients(level_gap):
    ratio_q = (center_depth + level_gap) * inverse_half
    root_term = jnp.sqrt(ratio_q * ratio_q - 1.0)
    decay = ratio_q - root_term
    first = -inverse_half / root_term
    series = [first]
    current = first * (-2.0 * decay)
    series.append(current)
    for offset in range(2, SWEEPS + 1):
        current = current * -decay
        series.append(current)
    return [term[:, None, None, None] for term in series]


def sweep_single(initial, veff, series):
    summed = series[0] * initial
    previous = initial
    current = initial
    for offset in range(1, SWEEPS + 1):
        image = apply_map(extended_2(current, (("dom", 1),), 3), veff)
        if offset == 1:
            following = image
        else:
            following = 2.0 * image - previous
        summed = summed + series[offset] * following
        previous = current
        current = following
    return summed


def per_device(orbitals, veff, trials, owners, levels, shift_index):
    grid_cells = orbitals.shape[1] * orbitals.shape[2] * orbitals.shape[3] * lax.axis_size("dom")
    orbital_count = orbitals.shape[0] * lax.axis_size("orb")
    chosen = shift_index[:, None] == jnp.arange(levels.shape[0], dtype=jnp.int32)[None, :]
    level_gaps = jnp.sum(jnp.where(chosen, levels[None, :], 0.0), axis=1)
    series = coefficients(level_gaps)
    potentials = []
    for app_index in range(APPS):
        received = spread(trials[0], "orb", owners[app_index])
        trial_total = lax.psum(jnp.sum(received * received), "dom")
        potentials.append(received * lax.rsqrt(trial_total / grid_cells + norm_epsilon))
    responses = []
    for app_index in range(APPS):
        deltas = sweep_single(potentials[app_index][None] * orbitals, veff, series)
        local_sum = jnp.sum(orbitals * deltas, axis=0)
        responses.append(lax.psum(local_sum, "orb"))
    my_group = lax.axis_index("orb")
    result = jnp.zeros(orbitals.shape[1:], jnp.float32)
    for app_index in range(APPS):
        response = responses[app_index] * (4.0 / orbital_count)
        result = result + jnp.where(owners[app_index] == my_group, response, 0.0)
    return result[None]


def solution(mesh):
    placed = (
        P("orb", "dom", None, None),
        P("dom", None, None),
        P("orb", "dom", None, None),
        P(),
        P(),
        P("orb"),
    )
    return jax.shard_map(
        per_device,
        mesh=mesh,
        in_specs=placed,
        out_specs=P("orb", "dom", None, None),
        check_vma=False,
    )
```

profile of v0, /device:TPU:1, one launch (start us, length us, event | category | flops | bytes accessed | tf_op | source)
XLA Modules:
  0.0 520.6 jit_solution(1561641401315790378)
XLA Ops:
  6.5 1.4 fusion.259
  9.2 1.8 select_bitcast_fusion.1
  12.0 120.3 %all-reduce.16.cloned.1.call-done = (f32[8,64,128]{2,1,0:T(8,128)}, f32[8,64,128]{2,1,0:T(8,128)}) async-done(((f32[8,64,128]{2,1,0:T(8,128)}, f32[8,64,128]{2,1,0:T(8,128)}), (f32[8,64,128]{2,1,0:T(8,128)}, f32[8,64,128]{2,1,0:T(8,128)})) %all-reduce.16.cloned.1.call-update) | async-done | bytes 524304 | tf_op jit(solution)/shard_map/psum | solution.py:30
  132.3 1.8 multiply_reduce_fusion
  134.1 20.7 %all-reduce.10 = (f32[]{:T(128)}, f32[]{:T(128)}) all-reduce(f32[]{:T(128)} %get-tuple-element.44, f32[]{:T(128)} %get-tuple-element.45), channel_id=1, replica_groups=mesh['orb'=16,'dom'=8] {'dom'}, use_global_device_ids=true, to_apply=%region_8.9 | all-reduce | flops 2 | bytes 16 | tf_op jit(solution)/shard_map/psum | solution.py:97
  159.0 1.4 collective-permute-start
  160.4 4.0 collective-permute-start.1
  165.2 1.4 fusion.258
  166.6 1.3 collective-permute-start.8
  167.9 4.9 collective-permute-start.9
  172.8 2.7 collective-permute-done
  177.3 3.5 select_maximum_fusion.14
  180.8 10.7 %broadcast_multiply_fusion.2 = (f32[8,8,64,128]{3,2,1,0:T(8,128)S(1)}, f32[8,8,64,128]{3,2,1,0:T(8,128)}) fusion(f32[8,8,64,128]{3,2,1,0:T(8,128)} %copy-done.10, f32[8,64,128]{2,1,0:T(8,128)S(1)} %copy-done.11, f32[8,14,70,134]{3,2,1,0:T(8,128)S(1)} %select_maximum_fusion.14, f32[8,3,64,128]{3,2,1,0:T(8,128)} %copy-done.16, f32[8,3,64,128]{3,2,1,0:T(8,128)} %copy-done.14), kind=kLoop, calls=%fused_computation.397 | loop fusion | flops 20971520 | bytes 33292288 | tf_op jit(solution)/shard_map/mul | solution.py:55
  191.5 1.5 fusion.253
  193.0 1.3 collective-permute-start.2
  194.2 5.6 %collective-permute-start.3 = (f32[8,3,64,128]{3,2,1,0:T(8,128)}, f32[8,3,64,128]{3,2,1,0:T(8,128)}, u32[]{:S(2)}, u32[]{:S(2)}) collective-permute-start(f32[8,3,64,128]{3,2,1,0:T(8,128)} %get-tuple-element.25), channel_id=1, source_target_pairs={{0,1},{1,2},{2,3},{3,4},{4,5},{5,6},{6,7},{8,9},{9,10},{10,11},{11... | collective-permute-start | bytes 2359304 | tf_op jit(solution)/shard_map/ppermute | solution.py:20
  199.9 4.6 select_maximum_fusion.6
  204.5 10.6 %broadcast_multiply_fusion.1 = (f32[8,8,64,128]{3,2,1,0:T(8,128)S(1)}, f32[8,8,64,128]{3,2,1,0:T(8,128)}) fusion(f32[8,8,64,128]{3,2,1,0:T(8,128)} %copy-done.9, f32[8,64,128]{2,1,0:T(8,128)S(1)} %copy-done.11, f32[8,14,70,134]{3,2,1,0:T(8,128)S(1)} %select_maximum_fusion.6, f32[8,3,64,128]{3,2,1,0:T(8,128)} %collective-permute-done.9, ...), kind=kLoop, calls=%fused_computation.396 | loop fusion | flops 20971520 | bytes 33292288 | tf_op jit(solution)/shard_map/mul | solution.py:55
  215.1 1.3 fusion.257
  216.4 1.4 collective-permute-start.10
  217.9 5.0 collective-permute-start.11
  222.9 4.8 select_maximum_fusion.12
  227.7 9.5 %fusion.152 = f32[8,8,64,128]{3,2,1,0:T(8,128)S(1)} fusion(f32[8,8,64,128]{3,2,1,0:T(8,128)} %copy-done.4, f32[8,3,64,128]{3,2,1,0:T(8,128)} %collective-permute-done.3, f32[8,3,64,128]{3,2,1,0:T(8,128)} %collective-permute-done.2, f32[8,14,70,134]{3,2,1,0:T(8,128)S(1)} %select_maximum_fusion.12, f32[8,8,64,128]{3,2,1,0:T(8,128)S(1)} %copy-done.2, ...), kind=kLoop, calls=%fused_computation.236 | loop fusion | flops 22020096 | bytes 35651584 | tf_op jit(solution)/shard_map/sub | solution.py:81
  237.2 1.4 fusion.252
  238.6 1.3 collective-permute-start.4
  239.9 5.0 collective-permute-start.5
  244.9 4.8 select_maximum_fusion.4
  249.7 9.7 %fusion.63 = f32[8,8,64,128]{3,2,1,0:T(8,128)S(1)} fusion(f32[8,8,64,128]{3,2,1,0:T(8,128)} %copy-done.6, f32[8,3,64,128]{3,2,1,0:T(8,128)} %collective-permute-done.11, f32[8,3,64,128]{3,2,1,0:T(8,128)} %collective-permute-done.10, f32[8,14,70,134]{3,2,1,0:T(8,128)S(1)} %select_maximum_fusion.4, f32[8,8,64,128]{3,2,1,0:T(8,128)} %get-tuple-element.19, ...), kind=kLoop, calls=%fused_computation.147 | loop fusion | flops 22020096 | bytes 35651584 | tf_op jit(solution)/shard_map/sub | solution.py:81
  259.4 1.5 fusion.256
  261.0 1.3 collective-permute-start.12
  262.3 4.9 collective-permute-start.13
  267.2 4.5 select_maximum_fusion.10
  271.7 8.6 %fusion.130 = f32[8,8,64,128]{3,2,1,0:T(8,128)} fusion(f32[8,8,64,128]{3,2,1,0:T(8,128)S(1)} %fusion.152, f32[8,3,64,128]{3,2,1,0:T(8,128)} %collective-permute-done.5, f32[8,3,64,128]{3,2,1,0:T(8,128)S(1)} %collective-permute-done.4, f32[8,14,70,134]{3,2,1,0:T(8,128)S(1)} %select_maximum_fusion.10, f32[8,64,128]{2,1,0:T(8,128)S(1)} %copy-done.11, ...), kind=kLoop, calls=%fused_computation.214 | loop fusion | flops 22020096 | bytes 33292288 | tf_op jit(solution)/shard_map/sub | solution.py:81
  280.3 2.7 fusion.251
  283.0 1.3 collective-permute-start.6
  284.3 7.1 %collective-permute-start.7 = (f32[8,3,64,128]{3,2,1,0:T(8,128)}, f32[8,3,64,128]{3,2,1,0:T(8,128)}, u32[]{:S(2)}, u32[]{:S(2)}) collective-permute-start(f32[8,3,64,128]{3,2,1,0:T(8,128)} %get-tuple-element.20), channel_id=1, source_target_pairs={{0,1},{1,2},{2,3},{3,4},{4,5},{5,6},{6,7},{8,9},{9,10},{10,11},{11... | collective-permute-start | bytes 2359304 | tf_op jit(solution)/shard_map/ppermute | solution.py:20
  291.4 4.8 select_maximum_fusion.2
  296.2 8.8 %fusion.41 = f32[8,8,64,128]{3,2,1,0:T(8,128)} fusion(f32[8,8,64,128]{3,2,1,0:T(8,128)S(1)} %fusion.63, f32[8,3,64,128]{3,2,1,0:T(8,128)} %collective-permute-done.13, f32[8,3,64,128]{3,2,1,0:T(8,128)} %collective-permute-done.12, f32[8,14,70,134]{3,2,1,0:T(8,128)S(1)} %select_maximum_fusion.2, f32[8,64,128]{2,1,0:T(8,128)S(1)} %copy-done.11, ...), kind=kLoop, calls=%fused_computation.125 | loop fusion | flops 22020096 | bytes 33292288 | tf_op jit(solution)/shard_map/sub | solution.py:81
  305.0 1.7 fusion.255
  306.7 1.3 collective-permute-start.14
  308.0 7.1 %collective-permute-start.15 = (f32[8,3,64,128]{3,2,1,0:T(8,128)S(1)}, f32[8,3,64,128]{3,2,1,0:T(8,128)S(1)}, u32[]{:S(2)}, u32[]{:S(2)}) collective-permute-start(f32[8,3,64,128]{3,2,1,0:T(8,128)S(1)} %get-tuple-element.30), channel_id=1, source_target_pairs={{0,1},{1,2},{2,3},{3,4},{4,5},{5,6},{6,7},{8,9},{9,10},{10,11},{11... | collective-permute-start | bytes 2359304 | tf_op jit(solution)/shard_map/ppermute | solution.py:20
  315.1 6.6 %select_maximum_fusion.8 = f32[8,14,70,134]{3,2,1,0:T(8,128)} fusion(f32[8,3,64,128]{3,2,1,0:T(8,128)S(1)} %collective-permute-done.6, f32[8,8,64,128]{3,2,1,0:T(8,128)S(1)} %copy-done.3, f32[8,3,64,128]{3,2,1,0:T(8,128)} %collective-permute-done.7), kind=kLoop, calls=%fused_computation.12 | loop fusion | flops 15758400 | bytes 7872256 | tf_op jit(solution)/shard_map/concatenate | solution.py:24
  322.1 1.6 collective-permute-done.15
  323.8 3.5 select_maximum_fusion
  327.3 28.0 %fusion.245 = f32[8,64,128]{2,1,0:T(8,128)} fusion(f32[8,8,64,128]{3,2,1,0:T(8,128)S(1)} %copy-done, f32[8,8,64,128]{3,2,1,0:T(8,128)S(1)} %fusion.152, f32[8,8,64,128]{3,2,1,0:T(8,128)} %fusion.130, f32[8,14,70,134]{3,2,1,0:T(8,128)} %select_maximum_fusion.8, f32[8,3,64,128]{3,2,1,0:T(8,128)} %collective-permute-done.7, f32[8,3,64,128]{3,2,1,0:T(8,128)} %copy-done.13, ...), kind=kLoop, calls=%fused_computation.393 | loop fusion | flops 27721728 | bytes 35913888 | tf_op jit(solution)/shard_map/reduce_sum | solution.py:102
  355.3 11.3 %fusion.246 = f32[8,64,128]{2,1,0:T(8,128)} fusion(f32[8,8,64,128]{3,2,1,0:T(8,128)S(1)} %copy-done, f32[8,8,64,128]{3,2,1,0:T(8,128)} %copy-done.1, f32[8,8,64,128]{3,2,1,0:T(8,128)} %fusion.41, f32[8,14,70,134]{3,2,1,0:T(8,128)S(1)} %select_maximum_fusion, f32[8,3,64,128]{3,2,1,0:T(8,128)} %copy-done.17, f32[8,3,64,128]{3,2,1,0:T(8,128)} %copy-done.15, ...), kind=kLoop, calls=%fused_computation.394 | loop fusion | flops 27721728 | bytes 35913888 | tf_op jit(solution)/shard_map/reduce_sum | solution.py:102
  367.9 144.0 %all-reduce.14.cloned.1.call-done = (f32[8,64,128]{2,1,0:T(8,128)}, f32[8,64,128]{2,1,0:T(8,128)}) async-done(((f32[8,64,128]{2,1,0:T(8,128)}, f32[8,64,128]{2,1,0:T(8,128)}), (f32[8,64,128]{2,1,0:T(8,128)}, f32[8,64,128]{2,1,0:T(8,128)})) %all-reduce.14.cloned.1.call-update) | async-done | bytes 524304 | tf_op jit(solution)/shard_map/psum | solution.py:103
  511.9 1.8 add_bitcast_fusion
  (64 shorter events, 6.7 us)
Async XLA Ops:
  6.5 151.6 %copy-start = (f32[8,8,64,128]{3,2,1,0:T(8,128)S(1)}, f32[8,8,64,128]{3,2,1,0:T(8,128)}, u32[]{:S(2)}) copy-start(f32[8,8,64,128]{3,2,1,0:T(8,128)} %param.6) | copy-start | bytes 6291460
  6.5 125.8 %all-reduce.16.cloned.1.call-start = ((), (), s32[]{:S(2)}) async-start(), calls=%async_computation.1 | async-start | bytes 1048576 | tf_op jit(solution)/shard_map/psum | solution.py:30
  11.1 500.9 %all-reduce.14.cloned.1.call-start = ((), (), s32[]{:S(2)}) async-start(), calls=%async_computation | async-start | bytes 1048576 | tf_op jit(solution)/shard_map/psum | solution.py:103
  158.1 0.8 copy-start.12
  158.9 17.6 %copy-start.10 = (f32[8,8,64,128]{3,2,1,0:T(8,128)}, f32[8,8,64,128]{3,2,1,0:T(8,128)S(1)}, u32[]{:S(2)}) copy-start(f32[8,8,64,128]{3,2,1,0:T(8,128)S(1)} %get-tuple-element.28) | copy-start | bytes 6291460
  158.9 41.0 %copy-start.9 = (f32[8,8,64,128]{3,2,1,0:T(8,128)}, f32[8,8,64,128]{3,2,1,0:T(8,128)S(1)}, u32[]{:S(2)}) copy-start(f32[8,8,64,128]{3,2,1,0:T(8,128)S(1)} %get-tuple-element.29) | copy-start | bytes 6291460
  158.9 5.6 %copy-start.11 = (f32[8,64,128]{2,1,0:T(8,128)S(1)}, f32[8,64,128]{2,1,0:T(8,128)}, u32[]{:S(2)}) copy-start(f32[8,64,128]{2,1,0:T(8,128)} %param.7) | copy-start | bytes 786436
  159.0 16.6 %collective-permute-start = (f32[8,3,64,128]{3,2,1,0:T(8,128)S(1)}, f32[8,3,64,128]{3,2,1,0:T(8,128)S(1)}, u32[]{:S(2)}, u32[]{:S(2)}) collective-permute-start(f32[8,3,64,128]{3,2,1,0:T(8,128)S(1)} %get-tuple-element.27), channel_id=1, source_target_pairs={{1,0},{2,1},{3,2},{4,3},{5,4},{6,5},{7,6},{9,8},{10,9},{11,10},{12... | collective-permute-start | bytes 2359304 | tf_op jit(solution)/shard_map/ppermute | solution.py:23
  160.4 16.0 %collective-permute-start.1 = (f32[8,3,64,128]{3,2,1,0:T(8,128)S(1)}, f32[8,3,64,128]{3,2,1,0:T(8,128)S(1)}, u32[]{:S(2)}, u32[]{:S(2)}) collective-permute-start(f32[8,3,64,128]{3,2,1,0:T(8,128)S(1)} %get-tuple-element.26), channel_id=1, source_target_pairs={{0,1},{1,2},{2,3},{3,4},{4,5},{5,6},{6,7},{8,9},{9,10},{10,11},{11... | collective-permute-start | bytes 2359304 | tf_op jit(solution)/shard_map/ppermute | solution.py:20
  166.6 33.3 %collective-permute-start.8 = (f32[8,3,64,128]{3,2,1,0:T(8,128)}, f32[8,3,64,128]{3,2,1,0:T(8,128)S(1)}, u32[]{:S(2)}, u32[]{:S(2)}) collective-permute-start(f32[8,3,64,128]{3,2,1,0:T(8,128)} %get-tuple-element.37), channel_id=1, source_target_pairs={{1,0},{2,1},{3,2},{4,3},{5,4},{6,5},{7,6},{9,8},{10,9},{11,10},{12... | collective-permute-start | bytes 2359304 | tf_op jit(solution)/shard_map/ppermute | solution.py:23
  167.9 32.0 %collective-permute-start.9 = (f32[8,3,64,128]{3,2,1,0:T(8,128)}, f32[8,3,64,128]{3,2,1,0:T(8,128)}, u32[]{:S(2)}, u32[]{:S(2)}) collective-permute-start(f32[8,3,64,128]{3,2,1,0:T(8,128)} %get-tuple-element.36), channel_id=1, source_target_pairs={{0,1},{1,2},{2,3},{3,4},{4,5},{5,6},{6,7},{8,9},{9,10},{10,11},{11... | collective-permute-start | bytes 2359304 | tf_op jit(solution)/shard_map/ppermute | solution.py:20
  175.5 0.9 copy-start.14
  176.4 0.9 copy-start.16
  191.5 13.0 %copy-start.4 = (f32[8,8,64,128]{3,2,1,0:T(8,128)}, f32[8,8,64,128]{3,2,1,0:T(8,128)S(1)}, u32[]{:S(2)}) copy-start(f32[8,8,64,128]{3,2,1,0:T(8,128)S(1)} %get-tuple-element.11) | copy-start | bytes 6291460
  193.0 29.9 %collective-permute-start.2 = (f32[8,3,64,128]{3,2,1,0:T(8,128)}, f32[8,3,64,128]{3,2,1,0:T(8,128)}, u32[]{:S(2)}, u32[]{:S(2)}) collective-permute-start(f32[8,3,64,128]{3,2,1,0:T(8,128)} %get-tuple-element.24), channel_id=1, source_target_pairs={{1,0},{2,1},{3,2},{4,3},{5,4},{6,5},{7,6},{9,8},{10,9},{11,10},{12... | collective-permute-start | bytes 2359304 | tf_op jit(solution)/shard_map/ppermute | solution.py:23
  194.2 28.7 %collective-permute-start.3 = (f32[8,3,64,128]{3,2,1,0:T(8,128)}, f32[8,3,64,128]{3,2,1,0:T(8,128)}, u32[]{:S(2)}, u32[]{:S(2)}) collective-permute-start(f32[8,3,64,128]{3,2,1,0:T(8,128)} %get-tuple-element.25), channel_id=1, source_target_pairs={{0,1},{1,2},{2,3},{3,4},{4,5},{5,6},{6,7},{8,9},{9,10},{10,11},{11... | collective-permute-start | bytes 2359304 | tf_op jit(solution)/shard_map/ppermute | solution.py:20
  215.1 7.8 %copy-start.6 = (f32[8,8,64,128]{3,2,1,0:T(8,128)}, f32[8,8,64,128]{3,2,1,0:T(8,128)S(1)}, u32[]{:S(2)}) copy-start(f32[8,8,64,128]{3,2,1,0:T(8,128)S(1)} %get-tuple-element.18) | copy-start | bytes 6291460
  215.1 7.8 %copy-start.5 = (f32[8,8,64,128]{3,2,1,0:T(8,128)S(1)}, f32[8,8,64,128]{3,2,1,0:T(8,128)}, u32[]{:S(2)}) copy-start(f32[8,8,64,128]{3,2,1,0:T(8,128)} %copy-done.4) | copy-start | bytes 6291460
  216.4 28.5 %collective-permute-start.10 = (f32[8,3,64,128]{3,2,1,0:T(8,128)}, f32[8,3,64,128]{3,2,1,0:T(8,128)}, u32[]{:S(2)}, u32[]{:S(2)}) collective-permute-start(f32[8,3,64,128]{3,2,1,0:T(8,128)} %get-tuple-element.34), channel_id=1, source_target_pairs={{1,0},{2,1},{3,2},{4,3},{5,4},{6,5},{7,6},{9,8},{10,9},{11,10},{12... | collective-permute-start | bytes 2359304 | tf_op jit(solution)/shard_map/ppermute | solution.py:23
  217.8 9.9 %copy-start.2 = (f32[8,8,64,128]{3,2,1,0:T(8,128)S(1)}, f32[8,8,64,128]{3,2,1,0:T(8,128)}, u32[]{:S(2)}) copy-start(f32[8,8,64,128]{3,2,1,0:T(8,128)} %get-tuple-element.12) | copy-start | bytes 6291460
  217.9 27.0 %collective-permute-start.11 = (f32[8,3,64,128]{3,2,1,0:T(8,128)}, f32[8,3,64,128]{3,2,1,0:T(8,128)}, u32[]{:S(2)}, u32[]{:S(2)}) collective-permute-start(f32[8,3,64,128]{3,2,1,0:T(8,128)} %get-tuple-element.35), channel_id=1, source_target_pairs={{0,1},{1,2},{2,3},{3,4},{4,5},{5,6},{6,7},{8,9},{9,10},{10,11},{11... | collective-permute-start | bytes 2359304 | tf_op jit(solution)/shard_map/ppermute | solution.py:20
  237.2 7.7 %copy-start.7 = (f32[8,8,64,128]{3,2,1,0:T(8,128)S(1)}, f32[8,8,64,128]{3,2,1,0:T(8,128)}, u32[]{:S(2)}) copy-start(f32[8,8,64,128]{3,2,1,0:T(8,128)} %copy-done.6) | copy-start | bytes 6291460
  238.6 28.6 %collective-permute-start.4 = (f32[8,3,64,128]{3,2,1,0:T(8,128)}, f32[8,3,64,128]{3,2,1,0:T(8,128)S(1)}, u32[]{:S(2)}, u32[]{:S(2)}) collective-permute-start(f32[8,3,64,128]{3,2,1,0:T(8,128)} %get-tuple-element.22), channel_id=1, source_target_pairs={{1,0},{2,1},{3,2},{4,3},{5,4},{6,5},{7,6},{9,8},{10,9},{11,10},{12... | collective-permute-start | bytes 2359304 | tf_op jit(solution)/shard_map/ppermute | solution.py:23
  239.9 9.8 %copy-start.18 = (f32[8,64,128]{2,1,0:T(8,128)S(1)}, f32[8,64,128]{2,1,0:T(8,128)}, u32[]{:S(2)}) copy-start(f32[8,64,128]{2,1,0:T(8,128)} %broadcast_multiply_fusion.5) | copy-start | bytes 786436
  239.9 27.3 %collective-permute-start.5 = (f32[8,3,64,128]{3,2,1,0:T(8,128)}, f32[8,3,64,128]{3,2,1,0:T(8,128)}, u32[]{:S(2)}, u32[]{:S(2)}) collective-permute-start(f32[8,3,64,128]{3,2,1,0:T(8,128)} %get-tuple-element.23), channel_id=1, source_target_pairs={{0,1},{1,2},{2,3},{3,4},{4,5},{5,6},{6,7},{8,9},{9,10},{10,11},{11... | collective-permute-start | bytes 2359304 | tf_op jit(solution)/shard_map/ppermute | solution.py:20
  259.4 36.7 %copy-start.1 = (f32[8,8,64,128]{3,2,1,0:T(8,128)}, f32[8,8,64,128]{3,2,1,0:T(8,128)S(1)}, u32[]{:S(2)}) copy-start(f32[8,8,64,128]{3,2,1,0:T(8,128)S(1)} %fusion.63) | copy-start | bytes 6291460
  261.0 30.4 %collective-permute-start.12 = (f32[8,3,64,128]{3,2,1,0:T(8,128)}, f32[8,3,64,128]{3,2,1,0:T(8,128)}, u32[]{:S(2)}, u32[]{:S(2)}) collective-permute-start(f32[8,3,64,128]{3,2,1,0:T(8,128)} %get-tuple-element.32), channel_id=1, source_target_pairs={{1,0},{2,1},{3,2},{4,3},{5,4},{6,5},{7,6},{9,8},{10,9},{11,10},{12... | collective-permute-start | bytes 2359304 | tf_op jit(solution)/shard_map/ppermute | solution.py:23
  262.3 29.1 %collective-permute-start.13 = (f32[8,3,64,128]{3,2,1,0:T(8,128)}, f32[8,3,64,128]{3,2,1,0:T(8,128)}, u32[]{:S(2)}, u32[]{:S(2)}) collective-permute-start(f32[8,3,64,128]{3,2,1,0:T(8,128)} %get-tuple-element.33), channel_id=1, source_target_pairs={{0,1},{1,2},{2,3},{3,4},{4,5},{5,6},{6,7},{8,9},{9,10},{10,11},{11... | collective-permute-start | bytes 2359304 | tf_op jit(solution)/shard_map/ppermute | solution.py:20
  283.0 32.1 %collective-permute-start.6 = (f32[8,3,64,128]{3,2,1,0:T(8,128)}, f32[8,3,64,128]{3,2,1,0:T(8,128)S(1)}, u32[]{:S(2)}, u32[]{:S(2)}) collective-permute-start(f32[8,3,64,128]{3,2,1,0:T(8,128)} %get-tuple-element.21), channel_id=1, source_target_pairs={{1,0},{2,1},{3,2},{4,3},{5,4},{6,5},{7,6},{9,8},{10,9},{11,10},{12... | collective-permute-start | bytes 2359304 | tf_op jit(solution)/shard_map/ppermute | solution.py:23
  284.3 30.8 %collective-permute-start.7 = (f32[8,3,64,128]{3,2,1,0:T(8,128)}, f32[8,3,64,128]{3,2,1,0:T(8,128)}, u32[]{:S(2)}, u32[]{:S(2)}) collective-permute-start(f32[8,3,64,128]{3,2,1,0:T(8,128)} %get-tuple-element.20), channel_id=1, source_target_pairs={{0,1},{1,2},{2,3},{3,4},{4,5},{5,6},{6,7},{8,9},{9,10},{10,11},{11... | collective-permute-start | bytes 2359304 | tf_op jit(solution)/shard_map/ppermute | solution.py:20
  305.0 10.2 %copy-start.3 = (f32[8,8,64,128]{3,2,1,0:T(8,128)S(1)}, f32[8,8,64,128]{3,2,1,0:T(8,128)}, u32[]{:S(2)}) copy-start(f32[8,8,64,128]{3,2,1,0:T(8,128)} %fusion.130) | copy-start | bytes 6291460
  306.7 15.5 %collective-permute-start.14 = (f32[8,3,64,128]{3,2,1,0:T(8,128)S(1)}, f32[8,3,64,128]{3,2,1,0:T(8,128)S(1)}, u32[]{:S(2)}, u32[]{:S(2)}) collective-permute-start(f32[8,3,64,128]{3,2,1,0:T(8,128)S(1)} %get-tuple-element.31), channel_id=1, source_target_pairs={{1,0},{2,1},{3,2},{4,3},{5,4},{6,5},{7,6},{9,8},{10,9},{11,10},{12... | collective-permute-start | bytes 2359304 | tf_op jit(solution)/shard_map/ppermute | solution.py:23
  308.0 15.8 %copy-start.8 = (f32[8,8,64,128]{3,2,1,0:T(8,128)S(1)}, f32[8,8,64,128]{3,2,1,0:T(8,128)}, u32[]{:S(2)}) copy-start(f32[8,8,64,128]{3,2,1,0:T(8,128)} %fusion.41) | copy-start | bytes 6291460
  308.0 15.8 %collective-permute-start.15 = (f32[8,3,64,128]{3,2,1,0:T(8,128)S(1)}, f32[8,3,64,128]{3,2,1,0:T(8,128)S(1)}, u32[]{:S(2)}, u32[]{:S(2)}) collective-permute-start(f32[8,3,64,128]{3,2,1,0:T(8,128)S(1)} %get-tuple-element.30), channel_id=1, source_target_pairs={{0,1},{1,2},{2,3},{3,4},{4,5},{5,6},{6,7},{8,9},{9,10},{10,11},{11... | collective-permute-start | bytes 2359304 | tf_op jit(solution)/shard_map/ppermute | solution.py:20
  315.1 6.7 %copy-start.13 = (f32[8,3,64,128]{3,2,1,0:T(8,128)}, f32[8,3,64,128]{3,2,1,0:T(8,128)S(1)}, u32[]{:S(2)}) copy-start(f32[8,3,64,128]{3,2,1,0:T(8,128)S(1)} %collective-permute-done.6) | copy-start | bytes 2359300
  322.1 5.1 copy-start.15
  323.8 3.5 copy-start.17
Sparse Core Ops, SparseCore 0:
  11.2 121.0 all-reduce.15
  366.8 145.1 all-reduce.13
where the time goes:
time: 522 us; the launch traced here: 521 us
  waiting for transfers between devices  270 us (52%)
  other arithmetic  144 us (28%)
  starting transfers between devices  54.3 us (10%)
  blocking collectives  20.7 us (4%)
  between operations  17.7 us (3%)
  local copies, waits for them, and re-layouts  14.1 us (3%)
    psum x1, waiting for transfers between devices, per_device(): responses.append(lax.psum(local_sum, 'orb'))  144 us
    psum x1, waiting for transfers between devices, spread(): return lax.psum(jnp.where(mine, shard, jnp.zeros_like(shard)), axis)  120 us
    ppermute x8, starting transfers between devices, extended_2(): lax.ppermute(lax.slice_in_dim(block, block.shape[dim] - width, None, axis...  43.7 us
    reduce_sum x2, other arithmetic, per_device(): local_sum = jnp.sum(orbitals * deltas, axis=0)  39.4 us
    concatenate x8, other arithmetic, extended_2(): block = jnp.concatenate([low, block, high], axis=dim)  37.1 us
    sub x4, other arithmetic, sweep_single(): following = 2.0 * image - previous  36.6 us
    mul x2, other arithmetic, apply_map(): return (energy - center_shift * middle) * inverse_half  21.3 us
    psum x1, blocking collectives, per_device(): trial_total = lax.psum(jnp.sum(received * received), 'dom')  20.7 us
  transfers between devices with their start and end apart: 18, of which 6 were waited for; matrix products, arithmetic and copies ran while one was open for 20% of the time, Pallas kernels for 0%

commit v1 on v0

--- a/solution.py
+++ b/solution.py
@@ -100,7 +100,7 @@
     for app_index in range(APPS):
         deltas = sweep_single(potentials[app_index][None] * orbitals, veff, series)
         local_sum = jnp.sum(orbitals * deltas, axis=0)
-        responses.append(lax.psum(local_sum, "orb"))
+        responses.append(jnp.sum(lax.all_gather(local_sum, "orb"), axis=0))
     my_group = lax.axis_index("orb")
     result = jnp.zeros(orbitals.shape[1:], jnp.float32)
     for app_index in range(APPS):

time: 522 us -> 472 us (0.904)
  waiting for transfers between devices: 270 us -> 220 us
    psum x1 -> x0, waiting for transfers between devices: 144 us -> none  [per_device(): responses.append(lax.psum(local_sum, 'orb'))]
    all_gather x0 -> x2, waiting for transfers between devices: none -> 74.7 us  [per_device(): responses.append(jnp.sum(lax.all_gather(local_sum, 'orb'), axis=0))]
    reduce_sum x2, other arithmetic: 39.4 us -> 22.2 us  [per_device(): local_sum = jnp.sum(orbitals * deltas, axis=0)]
    ppermute x8, waiting for transfers between devices: 3.09 us -> 20 us  [extended_2(): lax.ppermute(lax.slice_in_dim(block, 0, width, axis=dim), axis, backward)]
    sub x4, other arithmetic: 36.6 us -> 51.4 us  [sweep_single(): following = 2.0 * image - previous]
  transfers between devices with their start and end apart: 18 -> 19, of which waited for: 6 -> 11; matrix products, arithmetic and copies ran while one was open for 20% -> 20% of each run, Pallas kernels for 0% -> 0%
where the time goes in v1:
time: 472 us; the launch traced here: 471 us
  waiting for transfers between devices  220 us (47%)
  other arithmetic  142 us (30%)
  starting transfers between devices  54.4 us (12%)
  blocking collectives  20.7 us (4%)
  between operations  17.5 us (4%)
  local copies, waits for them, and re-layouts  15.8 us (3%)
    psum x1, waiting for transfers between devices, spread(): return lax.psum(jnp.where(mine, shard, jnp.zeros_like(shard)), axis)  120 us
    all_gather x2, waiting for transfers between devices, per_device(): responses.append(jnp.sum(lax.all_gather(local_sum, 'orb'), axis=0))  74.7 us
    sub x4, other arithmetic, sweep_single(): following = 2.0 * image - previous  51.4 us
    ppermute x8, starting transfers between devices, extended_2(): lax.ppermute(lax.slice_in_dim(block, block.shape[dim] - width, None, axis...  43.6 us
    concatenate x8, other arithmetic, extended_2(): block = jnp.concatenate([low, block, high], axis=dim)  35.8 us
    reduce_sum x2, other arithmetic, per_device(): local_sum = jnp.sum(orbitals * deltas, axis=0)  22.2 us
    psum x1, blocking collectives, per_device(): trial_total = lax.psum(jnp.sum(received * received), 'dom')  20.7 us
    ppermute x8, waiting for transfers between devices, extended_2(): lax.ppermute(lax.slice_in_dim(block, 0, width, axis=dim), axis, backward)  20 us
  transfers between devices with their start and end apart: 19, of which 11 were waited for; matrix products, arithmetic and copies ran while one was open for 20% of the time, Pallas kernels for 0%

profile of v1, /device:TPU:1, one launch (start us, length us, event | category | flops | bytes accessed | tf_op | source)
XLA Modules:
  0.0 470.5 jit_solution(9226022619124247587)
XLA Ops:
  6.5 1.4 fusion.259
  9.3 1.8 select_bitcast_fusion.1
  12.0 120.3 %all-reduce.12.cloned.1.call-done = (f32[8,64,128]{2,1,0:T(8,128)}, f32[8,64,128]{2,1,0:T(8,128)}) async-done(((f32[8,64,128]{2,1,0:T(8,128)}, f32[8,64,128]{2,1,0:T(8,128)}), (f32[8,64,128]{2,1,0:T(8,128)}, f32[8,64,128]{2,1,0:T(8,128)})) %all-reduce.12.cloned.1.call-update) | async-done | bytes 524304 | tf_op jit(solution)/shard_map/psum | solution.py:30
  132.3 1.8 multiply_reduce_fusion
  134.1 20.7 %all-reduce.9 = (f32[]{:T(128)}, f32[]{:T(128)}) all-reduce(f32[]{:T(128)} %get-tuple-element.42, f32[]{:T(128)} %get-tuple-element.43), channel_id=1, replica_groups=mesh['orb'=16,'dom'=8] {'dom'}, use_global_device_ids=true, to_apply=%region_8.9 | all-reduce | flops 2 | bytes 16 | tf_op jit(solution)/shard_map/psum | solution.py:97
  159.0 1.4 collective-permute-start
  160.4 4.0 collective-permute-start.1
  165.2 1.3 fusion.258
  167.9 4.9 %collective-permute-start.9 = (f32[8,3,64,128]{3,2,1,0:T(8,128)}, f32[8,3,64,128]{3,2,1,0:T(8,128)}, u32[]{:S(2)}, u32[]{:S(2)}) collective-permute-start(f32[8,3,64,128]{3,2,1,0:T(8,128)} %get-tuple-element.34), channel_id=1, source_target_pairs={{0,1},{1,2},{2,3},{3,4},{4,5},{5,6},{6,7},{8,9},{9,10},{10,11},{11... | collective-permute-start | bytes 2359304 | tf_op jit(solution)/shard_map/ppermute | solution.py:20
  172.7 2.8 collective-permute-done
  177.3 3.5 select_maximum_fusion.14
  180.9 10.7 %broadcast_multiply_fusion.2 = (f32[8,8,64,128]{3,2,1,0:T(8,128)S(1)}, f32[8,8,64,128]{3,2,1,0:T(8,128)}) fusion(f32[8,8,64,128]{3,2,1,0:T(8,128)} %copy-done.10, f32[8,64,128]{2,1,0:T(8,128)S(1)} %copy-done.11, f32[8,14,70,134]{3,2,1,0:T(8,128)S(1)} %select_maximum_fusion.14, f32[8,3,64,128]{3,2,1,0:T(8,128)} %copy-done.14, f32[8,3,64,128]{3,2,1,0:T(8,128)} %copy-done.13), kind=kLoop, calls=%fused_computation.397 | loop fusion | flops 20971520 | bytes 33292288 | tf_op jit(solution)/shard_map/mul | solution.py:55
  191.6 1.5 fusion.253
  194.4 5.6 %collective-permute-start.3 = (f32[8,3,64,128]{3,2,1,0:T(8,128)}, f32[8,3,64,128]{3,2,1,0:T(8,128)}, u32[]{:S(2)}, u32[]{:S(2)}) collective-permute-start(f32[8,3,64,128]{3,2,1,0:T(8,128)} %get-tuple-element.23), channel_id=1, source_target_pairs={{0,1},{1,2},{2,3},{3,4},{4,5},{5,6},{6,7},{8,9},{9,10},{10,11},{11... | collective-permute-start | bytes 2359304 | tf_op jit(solution)/shard_map/ppermute | solution.py:20
  200.0 4.6 select_maximum_fusion.6
  204.6 8.4 %broadcast_multiply_fusion.1 = (f32[8,8,64,128]{3,2,1,0:T(8,128)S(1)}, f32[8,8,64,128]{3,2,1,0:T(8,128)}) fusion(f32[8,8,64,128]{3,2,1,0:T(8,128)S(1)} %get-tuple-element.27, f32[8,64,128]{2,1,0:T(8,128)S(1)} %copy-done.11, f32[8,14,70,134]{3,2,1,0:T(8,128)S(1)} %select_maximum_fusion.6, f32[8,3,64,128]{3,2,1,0:T(8,128)} %collective-permute-done.9, ...), kind=kLoop, calls=%fused_computation.396 | loop fusion | flops 20971520 | bytes 33292288 | tf_op jit(solution)/shard_map/mul | solution.py:55
  213.0 1.3 fusion.257
  214.3 1.4 collective-permute-start.10
  215.7 5.0 %collective-permute-start.11 = (f32[8,3,64,128]{3,2,1,0:T(8,128)}, f32[8,3,64,128]{3,2,1,0:T(8,128)}, u32[]{:S(2)}, u32[]{:S(2)}) collective-permute-start(f32[8,3,64,128]{3,2,1,0:T(8,128)} %get-tuple-element.33), channel_id=1, source_target_pairs={{0,1},{1,2},{2,3},{3,4},{4,5},{5,6},{6,7},{8,9},{9,10},{10,11},{11... | collective-permute-start | bytes 2359304 | tf_op jit(solution)/shard_map/ppermute | solution.py:20
  220.8 4.8 %select_maximum_fusion.12 = f32[8,14,70,134]{3,2,1,0:T(8,128)S(1)} fusion(f32[8,3,64,128]{3,2,1,0:T(8,128)} %collective-permute-done.2, f32[8,8,64,128]{3,2,1,0:T(8,128)S(1)} %copy-done.8, f32[8,3,64,128]{3,2,1,0:T(8,128)} %collective-permute-done.3), kind=kLoop, calls=%fused_computation.16 | loop fusion | flops 15758400 | bytes 7872256 | tf_op jit(solution)/shard_map/concatenate | solution.py:24
  225.6 9.6 %fusion.152 = f32[8,8,64,128]{3,2,1,0:T(8,128)S(1)} fusion(f32[8,8,64,128]{3,2,1,0:T(8,128)} %copy-done.7, f32[8,3,64,128]{3,2,1,0:T(8,128)} %collective-permute-done.3, f32[8,3,64,128]{3,2,1,0:T(8,128)} %collective-permute-done.2, f32[8,14,70,134]{3,2,1,0:T(8,128)S(1)} %select_maximum_fusion.12, f32[8,8,64,128]{3,2,1,0:T(8,128)S(1)} %copy-done.4, ...), kind=kLoop, calls=%fused_computation.236 | loop fusion | flops 22020096 | bytes 35651584 | tf_op jit(solution)/shard_map/sub | solution.py:81
  235.3 1.4 collective-permute-start.4
  236.8 4.2 collective-permute-start.5
  241.0 4.8 %select_maximum_fusion.4 = f32[8,14,70,134]{3,2,1,0:T(8,128)S(1)} fusion(f32[8,3,64,128]{3,2,1,0:T(8,128)} %collective-permute-done.10, f32[8,8,64,128]{3,2,1,0:T(8,128)S(1)} %copy-done.6, f32[8,3,64,128]{3,2,1,0:T(8,128)} %collective-permute-done.11), kind=kLoop, calls=%fused_computation.8 | loop fusion | flops 15758400 | bytes 7872256 | tf_op jit(solution)/shard_map/concatenate | solution.py:24
  245.8 2.4 collective-permute-done.4
  248.2 1.5 collective-permute-done.5
  250.6 6.0 %select_maximum_fusion.10 = f32[8,14,70,134]{3,2,1,0:T(8,128)} fusion(f32[8,3,64,128]{3,2,1,0:T(8,128)S(1)} %collective-permute-done.4, f32[8,8,64,128]{3,2,1,0:T(8,128)S(1)} %fusion.152, f32[8,3,64,128]{3,2,1,0:T(8,128)S(1)} %collective-permute-done.5), kind=kLoop, calls=%fused_computation.14 | loop fusion | flops 15758400 | bytes 7872256 | tf_op jit(solution)/shard_map/concatenate | solution.py:24
  256.6 23.1 %fusion.130 = f32[8,8,64,128]{3,2,1,0:T(8,128)} fusion(f32[8,8,64,128]{3,2,1,0:T(8,128)S(1)} %fusion.152, f32[8,3,64,128]{3,2,1,0:T(8,128)} %copy-done.17, f32[8,3,64,128]{3,2,1,0:T(8,128)S(1)} %collective-permute-done.4, f32[8,14,70,134]{3,2,1,0:T(8,128)} %select_maximum_fusion.10, f32[8,64,128]{2,1,0:T(8,128)S(1)} %copy-done.11, ...), kind=kLoop, calls=%fused_computation.214 | loop fusion | flops 22020096 | bytes 33292288 | tf_op jit(solution)/shard_map/sub | solution.py:81
  279.7 2.9 fusion.251
  283.9 5.3 %collective-permute-start.7 = (f32[8,3,64,128]{3,2,1,0:T(8,128)}, f32[8,3,64,128]{3,2,1,0:T(8,128)}, u32[]{:S(2)}, u32[]{:S(2)}) collective-permute-start(f32[8,3,64,128]{3,2,1,0:T(8,128)} %get-tuple-element.18), channel_id=1, source_target_pairs={{0,1},{1,2},{2,3},{3,4},{4,5},{5,6},{6,7},{8,9},{9,10},{10,11},{11... | collective-permute-start | bytes 2359304 | tf_op jit(solution)/shard_map/ppermute | solution.py:20
  289.2 10.3 %fusion.63 = f32[8,8,64,128]{3,2,1,0:T(8,128)} fusion(f32[8,8,64,128]{3,2,1,0:T(8,128)} %copy-done.5, f32[8,3,64,128]{3,2,1,0:T(8,128)} %collective-permute-done.11, f32[8,3,64,128]{3,2,1,0:T(8,128)} %collective-permute-done.10, f32[8,14,70,134]{3,2,1,0:T(8,128)S(1)} %select_maximum_fusion.4, f32[8,8,64,128]{3,2,1,0:T(8,128)S(1)} %copy-done.2, ...), kind=kLoop, calls=%fused_computation.147 | loop fusion | flops 22020096 | bytes 35651584 | tf_op jit(solution)/shard_map/sub | solution.py:81
  299.5 5.2 %select_maximum_fusion.8 = f32[8,14,70,134]{3,2,1,0:T(8,128)S(1)} fusion(f32[8,3,64,128]{3,2,1,0:T(8,128)S(1)} %collective-permute-done.6, f32[8,8,64,128]{3,2,1,0:T(8,128)} %fusion.130, f32[8,3,64,128]{3,2,1,0:T(8,128)} %collective-permute-done.7), kind=kLoop, calls=%fused_computation.12 | loop fusion | flops 15758400 | bytes 7872256 | tf_op jit(solution)/shard_map/concatenate | solution.py:24
  304.7 11.0 %fusion.245 = f32[8,64,128]{2,1,0:T(8,128)} fusion(f32[8,8,64,128]{3,2,1,0:T(8,128)S(1)} %copy-done, f32[8,8,64,128]{3,2,1,0:T(8,128)S(1)} %fusion.152, f32[8,8,64,128]{3,2,1,0:T(8,128)} %fusion.130, f32[8,14,70,134]{3,2,1,0:T(8,128)S(1)} %select_maximum_fusion.8, f32[8,3,64,128]{3,2,1,0:T(8,128)} %collective-permute-done.7, ...), kind=kLoop, calls=%fused_computation.393 | loop fusion | flops 27721728 | bytes 35913888 | tf_op jit(solution)/shard_map/reduce_sum | solution.py:102
  315.8 1.7 fusion.256
  318.8 6.8 %collective-permute-start.13 = (f32[8,3,64,128]{3,2,1,0:T(8,128)S(1)}, f32[8,3,64,128]{3,2,1,0:T(8,128)S(1)}, u32[]{:S(2)}, u32[]{:S(2)}) collective-permute-start(f32[8,3,64,128]{3,2,1,0:T(8,128)S(1)} %get-tuple-element.31), channel_id=1, source_target_pairs={{0,1},{1,2},{2,3},{3,4},{4,5},{5,6},{6,7},{8,9},{9,10},{10,11},{11... | collective-permute-start | bytes 2359304 | tf_op jit(solution)/shard_map/ppermute | solution.py:20
  325.6 7.0 %collective-permute-done.12 = f32[8,3,64,128]{3,2,1,0:T(8,128)S(1)} collective-permute-done((f32[8,3,64,128]{3,2,1,0:T(8,128)S(1)}, f32[8,3,64,128]{3,2,1,0:T(8,128)S(1)}, u32[]{:S(2)}, u32[]{:S(2)}) %collective-permute-start.12) | collective-permute-done | bytes 786464 | tf_op jit(solution)/shard_map/ppermute | solution.py:23
  332.7 1.6 collective-permute-done.13
  335.1 3.5 select_maximum_fusion.2
  338.7 8.4 %fusion.41 = f32[8,8,64,128]{3,2,1,0:T(8,128)} fusion(f32[8,8,64,128]{3,2,1,0:T(8,128)S(1)} %copy-done.1, f32[8,3,64,128]{3,2,1,0:T(8,128)} %copy-done.19, f32[8,3,64,128]{3,2,1,0:T(8,128)S(1)} %collective-permute-done.12, f32[8,14,70,134]{3,2,1,0:T(8,128)S(1)} %select_maximum_fusion.2, f32[8,64,128]{2,1,0:T(8,128)S(1)} %copy-done.11, ...), kind=kLoop, calls=%fused_computation.125 | loop fusion | flops 22020096 | bytes 33292288 | tf_op jit(solution)/shard_map/sub | solution.py:81
  347.1 1.7 fusion.255
  350.1 7.6 %collective-permute-start.15 = (f32[8,3,64,128]{3,2,1,0:T(8,128)S(1)}, f32[8,3,64,128]{3,2,1,0:T(8,128)S(1)}, u32[]{:S(2)}, u32[]{:S(2)}) collective-permute-start(f32[8,3,64,128]{3,2,1,0:T(8,128)S(1)} %get-tuple-element.28), channel_id=1, source_target_pairs={{0,1},{1,2},{2,3},{3,4},{4,5},{5,6},{6,7},{8,9},{9,10},{10,11},{11... | collective-permute-start | bytes 2359304 | tf_op jit(solution)/shard_map/ppermute | solution.py:20
  357.8 7.8 %collective-permute-done.14 = f32[8,3,64,128]{3,2,1,0:T(8,128)S(1)} collective-permute-done((f32[8,3,64,128]{3,2,1,0:T(8,128)S(1)}, f32[8,3,64,128]{3,2,1,0:T(8,128)S(1)}, u32[]{:S(2)}, u32[]{:S(2)}) %collective-permute-start.14) | collective-permute-done | bytes 786464 | tf_op jit(solution)/shard_map/ppermute | solution.py:23
  367.5 3.5 select_maximum_fusion
  371.0 11.2 %fusion.246 = f32[8,64,128]{2,1,0:T(8,128)} fusion(f32[8,8,64,128]{3,2,1,0:T(8,128)S(1)} %copy-done, f32[8,8,64,128]{3,2,1,0:T(8,128)S(1)} %copy-done.1, f32[8,8,64,128]{3,2,1,0:T(8,128)} %fusion.41, f32[8,14,70,134]{3,2,1,0:T(8,128)S(1)} %select_maximum_fusion, f32[8,3,64,128]{3,2,1,0:T(8,128)} %copy-done.18, f32[8,3,64,128]{3,2,1,0:T(8,128)} %copy-done.16, ...), kind=kLoop, calls=%fused_computation.394 | loop fusion | flops 27721728 | bytes 35913888 | tf_op jit(solution)/shard_map/reduce_sum | solution.py:102
  383.6 23.9 %all-gather.5.cloned.1.call-done = f32[128,64,128]{2,1,0:T(8,128)} async-done(((f32[8,64,128]{2,1,0:T(8,128)}), f32[128,64,128]{2,1,0:T(8,128)}) %all-gather.5.cloned.1.call-update) | async-done | bytes 4194320 | tf_op jit(solution)/shard_map/all_gather | solution.py:103
  407.4 2.5 reduce_sum.66
  409.9 50.9 %all-gather.7.cloned.1.call-done = f32[128,64,128]{2,1,0:T(8,128)} async-done(((f32[8,64,128]{2,1,0:T(8,128)}), f32[128,64,128]{2,1,0:T(8,128)}) %all-gather.7.cloned.1.call-update) | async-done | bytes 4194320 | tf_op jit(solution)/shard_map/all_gather | solution.py:103
  460.8 2.5 reduce_sum.69
  (73 shorter events, 17.4 us)
Async XLA Ops:
  6.5 151.6 %copy-start = (f32[8,8,64,128]{3,2,1,0:T(8,128)S(1)}, f32[8,8,64,128]{3,2,1,0:T(8,128)}, u32[]{:S(2)}) copy-start(f32[8,8,64,128]{3,2,1,0:T(8,128)} %param.6) | copy-start | bytes 6291460
  6.5 125.8 %all-reduce.12.cloned.1.call-start = ((), (), s32[]{:S(2)}) async-start(), calls=%async_computation.2 | async-start | bytes 1048576 | tf_op jit(solution)/shard_map/psum | solution.py:30
  11.1 396.3 %all-gather.5.cloned.1.call-start = ((), (), s32[]{:S(2)}) async-start(), calls=%async_computation | async-start | bytes 4456448 | tf_op jit(solution)/shard_map/all_gather | solution.py:103
  158.1 0.8 copy-start.12
  158.9 17.6 %copy-start.10 = (f32[8,8,64,128]{3,2,1,0:T(8,128)}, f32[8,8,64,128]{3,2,1,0:T(8,128)S(1)}, u32[]{:S(2)}) copy-start(f32[8,8,64,128]{3,2,1,0:T(8,128)S(1)} %get-tuple-element.26) | copy-start | bytes 6291460
  158.9 5.6 %copy-start.11 = (f32[8,64,128]{2,1,0:T(8,128)S(1)}, f32[8,64,128]{2,1,0:T(8,128)}, u32[]{:S(2)}) copy-start(f32[8,64,128]{2,1,0:T(8,128)} %param.7) | copy-start | bytes 786436
  159.0 16.6 %collective-permute-start = (f32[8,3,64,128]{3,2,1,0:T(8,128)S(1)}, f32[8,3,64,128]{3,2,1,0:T(8,128)S(1)}, u32[]{:S(2)}, u32[]{:S(2)}) collective-permute-start(f32[8,3,64,128]{3,2,1,0:T(8,128)S(1)} %get-tuple-element.25), channel_id=1, source_target_pairs={{1,0},{2,1},{3,2},{4,3},{5,4},{6,5},{7,6},{9,8},{10,9},{11,10},{12... | collective-permute-start | bytes 2359304 | tf_op jit(solution)/shard_map/ppermute | solution.py:23
  160.4 16.0 %collective-permute-start.1 = (f32[8,3,64,128]{3,2,1,0:T(8,128)S(1)}, f32[8,3,64,128]{3,2,1,0:T(8,128)S(1)}, u32[]{:S(2)}, u32[]{:S(2)}) collective-permute-start(f32[8,3,64,128]{3,2,1,0:T(8,128)S(1)} %get-tuple-element.24), channel_id=1, source_target_pairs={{0,1},{1,2},{2,3},{3,4},{4,5},{5,6},{6,7},{8,9},{9,10},{10,11},{11... | collective-permute-start | bytes 2359304 | tf_op jit(solution)/shard_map/ppermute | solution.py:20
  166.6 33.5 %collective-permute-start.8 = (f32[8,3,64,128]{3,2,1,0:T(8,128)}, f32[8,3,64,128]{3,2,1,0:T(8,128)S(1)}, u32[]{:S(2)}, u32[]{:S(2)}) collective-permute-start(f32[8,3,64,128]{3,2,1,0:T(8,128)} %get-tuple-element.35), channel_id=1, source_target_pairs={{1,0},{2,1},{3,2},{4,3},{5,4},{6,5},{7,6},{9,8},{10,9},{11,10},{12... | collective-permute-start | bytes 2359304 | tf_op jit(solution)/shard_map/ppermute | solution.py:23
  167.9 32.2 %collective-permute-start.9 = (f32[8,3,64,128]{3,2,1,0:T(8,128)}, f32[8,3,64,128]{3,2,1,0:T(8,128)}, u32[]{:S(2)}, u32[]{:S(2)}) collective-permute-start(f32[8,3,64,128]{3,2,1,0:T(8,128)} %get-tuple-element.34), channel_id=1, source_target_pairs={{0,1},{1,2},{2,3},{3,4},{4,5},{5,6},{6,7},{8,9},{9,10},{10,11},{11... | collective-permute-start | bytes 2359304 | tf_op jit(solution)/shard_map/ppermute | solution.py:20
  175.5 0.9 copy-start.13
  176.4 0.9 copy-start.14
  191.6 8.4 %copy-start.7 = (f32[8,8,64,128]{3,2,1,0:T(8,128)}, f32[8,8,64,128]{3,2,1,0:T(8,128)S(1)}, u32[]{:S(2)}) copy-start(f32[8,8,64,128]{3,2,1,0:T(8,128)S(1)} %get-tuple-element.9) | copy-start | bytes 6291460
  193.1 27.7 %collective-permute-start.2 = (f32[8,3,64,128]{3,2,1,0:T(8,128)}, f32[8,3,64,128]{3,2,1,0:T(8,128)}, u32[]{:S(2)}, u32[]{:S(2)}) collective-permute-start(f32[8,3,64,128]{3,2,1,0:T(8,128)} %get-tuple-element.22), channel_id=1, source_target_pairs={{1,0},{2,1},{3,2},{4,3},{5,4},{6,5},{7,6},{9,8},{10,9},{11,10},{12... | collective-permute-start | bytes 2359304 | tf_op jit(solution)/shard_map/ppermute | solution.py:23
  194.4 26.4 %collective-permute-start.3 = (f32[8,3,64,128]{3,2,1,0:T(8,128)}, f32[8,3,64,128]{3,2,1,0:T(8,128)}, u32[]{:S(2)}, u32[]{:S(2)}) collective-permute-start(f32[8,3,64,128]{3,2,1,0:T(8,128)} %get-tuple-element.23), channel_id=1, source_target_pairs={{0,1},{1,2},{2,3},{3,4},{4,5},{5,6},{6,7},{8,9},{9,10},{10,11},{11... | collective-permute-start | bytes 2359304 | tf_op jit(solution)/shard_map/ppermute | solution.py:20
  213.0 7.8 %copy-start.5 = (f32[8,8,64,128]{3,2,1,0:T(8,128)}, f32[8,8,64,128]{3,2,1,0:T(8,128)S(1)}, u32[]{:S(2)}) copy-start(f32[8,8,64,128]{3,2,1,0:T(8,128)S(1)} %get-tuple-element.16) | copy-start | bytes 6291460
  213.0 7.8 %copy-start.8 = (f32[8,8,64,128]{3,2,1,0:T(8,128)S(1)}, f32[8,8,64,128]{3,2,1,0:T(8,128)}, u32[]{:S(2)}) copy-start(f32[8,8,64,128]{3,2,1,0:T(8,128)} %copy-done.7) | copy-start | bytes 6291460
  214.3 26.7 %collective-permute-start.10 = (f32[8,3,64,128]{3,2,1,0:T(8,128)}, f32[8,3,64,128]{3,2,1,0:T(8,128)}, u32[]{:S(2)}, u32[]{:S(2)}) collective-permute-start(f32[8,3,64,128]{3,2,1,0:T(8,128)} %get-tuple-element.32), channel_id=1, source_target_pairs={{1,0},{2,1},{3,2},{4,3},{5,4},{6,5},{7,6},{9,8},{10,9},{11,10},{12... | collective-permute-start | bytes 2359304 | tf_op jit(solution)/shard_map/ppermute | solution.py:23
  215.7 9.9 %copy-start.4 = (f32[8,8,64,128]{3,2,1,0:T(8,128)S(1)}, f32[8,8,64,128]{3,2,1,0:T(8,128)}, u32[]{:S(2)}) copy-start(f32[8,8,64,128]{3,2,1,0:T(8,128)} %get-tuple-element.10) | copy-start | bytes 6291460
  215.7 25.3 %collective-permute-start.11 = (f32[8,3,64,128]{3,2,1,0:T(8,128)}, f32[8,3,64,128]{3,2,1,0:T(8,128)}, u32[]{:S(2)}, u32[]{:S(2)}) collective-permute-start(f32[8,3,64,128]{3,2,1,0:T(8,128)} %get-tuple-element.33), channel_id=1, source_target_pairs={{0,1},{1,2},{2,3},{3,4},{4,5},{5,6},{6,7},{8,9},{9,10},{10,11},{11... | collective-permute-start | bytes 2359304 | tf_op jit(solution)/shard_map/ppermute | solution.py:20
  235.2 5.8 %copy-start.6 = (f32[8,8,64,128]{3,2,1,0:T(8,128)S(1)}, f32[8,8,64,128]{3,2,1,0:T(8,128)}, u32[]{:S(2)}) copy-start(f32[8,8,64,128]{3,2,1,0:T(8,128)} %copy-done.5) | copy-start | bytes 6291460
  235.3 12.9 %collective-permute-start.4 = (f32[8,3,64,128]{3,2,1,0:T(8,128)S(1)}, f32[8,3,64,128]{3,2,1,0:T(8,128)S(1)}, u32[]{:S(2)}, u32[]{:S(2)}) collective-permute-start(f32[8,3,64,128]{3,2,1,0:T(8,128)S(1)} %get-tuple-element.20), channel_id=1, source_target_pairs={{1,0},{2,1},{3,2},{4,3},{5,4},{6,5},{7,6},{9,8},{10,9},{11,10},{12... | collective-permute-start | bytes 2359304 | tf_op jit(solution)/shard_map/ppermute | solution.py:23
  236.8 12.9 %collective-permute-start.5 = (f32[8,3,64,128]{3,2,1,0:T(8,128)S(1)}, f32[8,3,64,128]{3,2,1,0:T(8,128)S(1)}, u32[]{:S(2)}, u32[]{:S(2)}) collective-permute-start(f32[8,3,64,128]{3,2,1,0:T(8,128)S(1)} %get-tuple-element.21), channel_id=1, source_target_pairs={{0,1},{1,2},{2,3},{3,4},{4,5},{5,6},{6,7},{8,9},{9,10},{10,11},{11... | collective-permute-start | bytes 2359304 | tf_op jit(solution)/shard_map/ppermute | solution.py:20
  249.7 0.9 copy-start.17
  279.7 9.5 %copy-start.2 = (f32[8,8,64,128]{3,2,1,0:T(8,128)S(1)}, f32[8,8,64,128]{3,2,1,0:T(8,128)}, u32[]{:S(2)}) copy-start(f32[8,8,64,128]{3,2,1,0:T(8,128)} %get-tuple-element.17) | copy-start | bytes 6291460
  279.7 9.5 %copy-start.20 = (f32[8,64,128]{2,1,0:T(8,128)S(1)}, f32[8,64,128]{2,1,0:T(8,128)}, u32[]{:S(2)}) copy-start(f32[8,64,128]{2,1,0:T(8,128)} %broadcast_multiply_fusion.5) | copy-start | bytes 786436
  282.6 16.9 %collective-permute-start.6 = (f32[8,3,64,128]{3,2,1,0:T(8,128)}, f32[8,3,64,128]{3,2,1,0:T(8,128)S(1)}, u32[]{:S(2)}, u32[]{:S(2)}) collective-permute-start(f32[8,3,64,128]{3,2,1,0:T(8,128)} %get-tuple-element.19), channel_id=1, source_target_pairs={{1,0},{2,1},{3,2},{4,3},{5,4},{6,5},{7,6},{9,8},{10,9},{11,10},{12... | collective-permute-start | bytes 2359304 | tf_op jit(solution)/shard_map/ppermute | solution.py:23
  283.9 15.6 %collective-permute-start.7 = (f32[8,3,64,128]{3,2,1,0:T(8,128)}, f32[8,3,64,128]{3,2,1,0:T(8,128)}, u32[]{:S(2)}, u32[]{:S(2)}) collective-permute-start(f32[8,3,64,128]{3,2,1,0:T(8,128)} %get-tuple-element.18), channel_id=1, source_target_pairs={{0,1},{1,2},{2,3},{3,4},{4,5},{5,6},{6,7},{8,9},{9,10},{10,11},{11... | collective-permute-start | bytes 2359304 | tf_op jit(solution)/shard_map/ppermute | solution.py:20
  299.5 5.2 %copy-start.15 = (f32[8,3,64,128]{3,2,1,0:T(8,128)}, f32[8,3,64,128]{3,2,1,0:T(8,128)S(1)}, u32[]{:S(2)}) copy-start(f32[8,3,64,128]{3,2,1,0:T(8,128)S(1)} %collective-permute-done.6) | copy-start | bytes 2359300
  315.7 145.0 %all-gather.7.cloned.1.call-start = ((), (), s32[]{:S(2)}) async-start(), calls=%async_computation.1 | async-start | bytes 4456448 | tf_op jit(solution)/shard_map/all_gather | solution.py:103
  315.8 19.4 %copy-start.1 = (f32[8,8,64,128]{3,2,1,0:T(8,128)S(1)}, f32[8,8,64,128]{3,2,1,0:T(8,128)}, u32[]{:S(2)}) copy-start(f32[8,8,64,128]{3,2,1,0:T(8,128)} %fusion.63) | copy-start | bytes 6291460
  317.5 15.2 %collective-permute-start.12 = (f32[8,3,64,128]{3,2,1,0:T(8,128)S(1)}, f32[8,3,64,128]{3,2,1,0:T(8,128)S(1)}, u32[]{:S(2)}, u32[]{:S(2)}) collective-permute-start(f32[8,3,64,128]{3,2,1,0:T(8,128)S(1)} %get-tuple-element.30), channel_id=1, source_target_pairs={{1,0},{2,1},{3,2},{4,3},{5,4},{6,5},{7,6},{9,8},{10,9},{11,10},{12... | collective-permute-start | bytes 2359304 | tf_op jit(solution)/shard_map/ppermute | solution.py:23
  318.8 19.9 %copy-start.3 = (f32[8,8,64,128]{3,2,1,0:T(8,128)S(1)}, f32[8,8,64,128]{3,2,1,0:T(8,128)}, u32[]{:S(2)}) copy-start(f32[8,8,64,128]{3,2,1,0:T(8,128)} %get-tuple-element.17) | copy-start | bytes 6291460
  318.8 15.5 %collective-permute-start.13 = (f32[8,3,64,128]{3,2,1,0:T(8,128)S(1)}, f32[8,3,64,128]{3,2,1,0:T(8,128)S(1)}, u32[]{:S(2)}, u32[]{:S(2)}) collective-permute-start(f32[8,3,64,128]{3,2,1,0:T(8,128)S(1)} %get-tuple-element.31), channel_id=1, source_target_pairs={{0,1},{1,2},{2,3},{3,4},{4,5},{5,6},{6,7},{8,9},{9,10},{10,11},{11... | collective-permute-start | bytes 2359304 | tf_op jit(solution)/shard_map/ppermute | solution.py:20
  334.3 0.9 copy-start.19
  347.1 20.4 %copy-start.9 = (f32[8,8,64,128]{3,2,1,0:T(8,128)S(1)}, f32[8,8,64,128]{3,2,1,0:T(8,128)}, u32[]{:S(2)}) copy-start(f32[8,8,64,128]{3,2,1,0:T(8,128)} %fusion.41) | copy-start | bytes 6291460
  348.8 16.7 %collective-permute-start.14 = (f32[8,3,64,128]{3,2,1,0:T(8,128)S(1)}, f32[8,3,64,128]{3,2,1,0:T(8,128)S(1)}, u32[]{:S(2)}, u32[]{:S(2)}) collective-permute-start(f32[8,3,64,128]{3,2,1,0:T(8,128)S(1)} %get-tuple-element.29), channel_id=1, source_target_pairs={{1,0},{2,1},{3,2},{4,3},{5,4},{6,5},{7,6},{9,8},{10,9},{11,10},{12... | collective-permute-start | bytes 2359304 | tf_op jit(solution)/shard_map/ppermute | solution.py:23
  350.1 16.5 %collective-permute-start.15 = (f32[8,3,64,128]{3,2,1,0:T(8,128)S(1)}, f32[8,3,64,128]{3,2,1,0:T(8,128)S(1)}, u32[]{:S(2)}, u32[]{:S(2)}) collective-permute-start(f32[8,3,64,128]{3,2,1,0:T(8,128)S(1)} %get-tuple-element.28), channel_id=1, source_target_pairs={{0,1},{1,2},{2,3},{3,4},{4,5},{5,6},{6,7},{8,9},{9,10},{10,11},{11... | collective-permute-start | bytes 2359304 | tf_op jit(solution)/shard_map/ppermute | solution.py:20
  365.6 1.1 copy-start.16
  366.6 0.9 copy-start.18
Sparse Core Ops, SparseCore 0:
  11.2 121.0 all-reduce.11
  315.9 91.5 all-gather.4
  409.2 51.4 all-gather.6
